TPU v7x, 32 devices: a whole 2x2x4 slice. The times are simulated.
32 devices in a mesh: dp: 2 (over x), row: 4 (over y, core), col: 4 (over z).
Axes of the slice: x: 2, y: 2, z: 4, core: 2. Of those that a mesh axis runs over, the one named last changes fastest.
Arguments:
- tokens: bfloat16 [896, 4096], P(('dp', 'col'), 'row'), may hold values from -6 to 6
- gate_up: bfloat16 [2, 4096, 14336], P(None, 'row', ('dp', 'col')), may hold values from -0.09375 to 0.09375
- down_weight: bfloat16 [14336, 4096], P(('dp', 'col'), 'row'), may hold values from -0.046875 to 0.046875
Outputs:
- mixed: bfloat16 [896, 4096], P(('dp', 'col'), 'row')
- col_check: float32 [4096], P('row')
- row_check: float32 [896], P(('dp', 'col'))
All inputs are finite; a program needn't handle non-finite values.
Results may differ from a plain program's by a relative error of at most 0.0049.
Values may be sent and summed in bfloat16 or wider, within the bound.
A program may use at most 128 MiB of HBM per device.

v0:
```python
import math

import jax
import jax.numpy as jnp
from jax import lax
from jax.sharding import PartitionSpec as P


def swiglu(partial_value):
    return (jax.nn.silu(partial_value[:, 0]) * partial_value[:, 1]).astype(jnp.bfloat16)


def hidden_units(partial_value):
    share = lax.psum_scatter(partial_value, "row", scatter_dimension=0, tiled=True)
    return lax.all_gather(swiglu(share), "row", axis=0, tiled=True)


def make_accumulate(hidden, shard_piece):
    columns_wide = hidden.astype(jnp.float32)
    piece_wide = shard_piece.astype(jnp.float32)
    output_part = jnp.dot(hidden, shard_piece, preferred_element_type=jnp.float32)
    column_part = jnp.dot(
        jnp.sum(columns_wide, axis=0), piece_wide, precision=lax.Precision.HIGHEST
    )
    row_part = jnp.dot(columns_wide, jnp.sum(piece_wide, axis=1), precision=lax.Precision.HIGHEST)
    return (output_part, column_part, row_part)


def per_device(tokens, gate_up, down_weight):
    total_tokens = tokens.shape[0] * lax.axis_size(("dp", "col"))
    model_width = tokens.shape[1] * lax.axis_size("row")
    group_rows = lax.all_gather(tokens, "col", axis=0, tiled=True)
    partial_value = jnp.einsum(
        "td,gdf->tgf",
        group_rows,
        lax.all_gather(gate_up, "dp", axis=2, tiled=True),
        preferred_element_type=jnp.float32,
    )
    hidden = hidden_units(partial_value)
    output_part, column_part, row_part = make_accumulate(
        hidden, lax.all_gather(down_weight, "dp", axis=0, tiled=True)
    )
    mixed, row_share = (
        lax.psum_scatter(output_part, "col", scatter_dimension=0, tiled=True),
        lax.psum_scatter(row_part, "col", scatter_dimension=0, tiled=True),
    )
    col_check = lax.psum(column_part, ("dp", "col")) / math.sqrt(total_tokens)
    row_check = lax.psum(row_share, "row") / math.sqrt(model_width)
    return (mixed.astype(jnp.bfloat16), col_check, row_check)


def solution(mesh):
    placed = (P(("dp", "col"), "row"), P(None, "row", ("dp", "col")), P(("dp", "col"), "row"))
    return jax.shard_map(
        per_device,
        mesh=mesh,
        in_specs=placed,
        out_specs=(P(("dp", "col"), "row"), P("row"), P(("dp", "col"))),
        check_vma=False,
    )
```

profile of v0, /device:TPU:0, one launch (start us, length us, event | category | flops | bytes accessed | tf_op | source)
XLA Modules:
  0.0 496.4 jit_solution(13311978647355852868)
XLA Ops:
  7.2 0.0 all-gather.4.cloned.1.call-start
  7.2 0.0 copy-start.1
  7.2 0.7 all-gather.4.cloned.1.call-update
  7.9 0.0 reduce-scatter.3.cloned.1.call-start
  7.9 0.2 copy-done.1
  8.2 22.7 %all_gather.12 = bf16[448,1024]{1,0:T(8,128)(2,1)S(1)} all-gather(bf16[112,1024]{1,0:T(8,128)(2,1)S(1)} %copy-done.1), channel_id=1, replica_groups=mesh['dp'=2,'row'=4,'col'=4] {'col'}, dimensions={0}, use_global_device_ids=true | all-gather | bytes 1146880 | tf_op jit(solution)/shard_map/all_gather | solution.py:32
  30.9 156.9 %all-gather.4.cloned.1.call-done = bf16[2,1024,3584]{2,1,0:T(8,128)(2,1)} async-done(((bf16[2,1024,1792]{2,1,0:T(8,128)(2,1)}), bf16[2,1024,3584]{2,1,0:T(8,128)(2,1)}) %all-gather.4.cloned.1.call-update) | async-done | bytes 14680080 | tf_op jit(solution)/shard_map/all_gather | solution.py:36
  187.8 14.9 %fusion.2 = f32[448,2,3584]{2,0,1:T(8,128)} fusion(bf16[2,1024,3584]{2,1,0:T(8,128)(2,1)} %all-gather.4.cloned.1.call-done, bf16[448,1024]{1,0:T(8,128)(2,1)S(1)} %all_gather.12), kind=kOutput, calls=%fused_computation.6 | convolution fusion | flops 6576668672 | bytes 28442624 | tf_op jit(solution)/shard_map/td,gdf->tgf/dot_general | solution.py:33
  202.7 0.0 reduce-scatter.3.cloned.1.call-update
  202.7 0.0 all-gather.8.cloned.1.call-start
  202.8 0.7 all-gather.8.cloned.1.call-update
  203.5 0.0 all-gather.6.cloned.1.call-start
  203.5 100.1 %reduce-scatter.3.cloned.1.call-done = f32[112,2,3584]{2,0,1:T(8,128)} async-done(((f32[448,2,3584]{2,0,1:T(8,128)}), f32[112,2,3584]{2,0,1:T(8,128)}) %reduce-scatter.3.cloned.1.call-update) | async-done | bytes 3211280 | tf_op jit(solution)/shard_map/reduce_scatter | solution.py:14
  303.6 3.2 fusion.1
  306.9 0.0 all-gather.6.cloned.1.call-update
  306.9 0.0 copy-start.2
  306.9 0.0 reduce-scatter.5.cloned.1.call-start
  307.0 90.5 %all-gather.8.cloned.1.call-done = bf16[3584,1024]{1,0:T(8,128)(2,1)} async-done(((bf16[1792,1024]{1,0:T(8,128)(2,1)}), bf16[3584,1024]{1,0:T(8,128)(2,1)}) %all-gather.8.cloned.1.call-update) | async-done | bytes 7340048 | tf_op jit(solution)/shard_map/all_gather | solution.py:41
  397.4 30.4 %all-gather.6.cloned.1.call-done = bf16[448,3584]{1,0:T(8,128)(2,1)} async-done(((bf16[112,3584]{1,0:T(8,128)(2,1)}), bf16[448,3584]{1,0:T(8,128)(2,1)}) %all-gather.6.cloned.1.call-update) | async-done | bytes 3211280 | tf_op jit(solution)/shard_map/all_gather | solution.py:15
  427.8 8.8 %fusion.4 = f32[448,1024]{1,0:T(8,128)} fusion(bf16[448,3584]{1,0:T(8,128)(2,1)} %all-gather.6.cloned.1.call-done, bf16[3584,1024]{1,0:T(8,128)(2,1)} %all-gather.8.cloned.1.call-done), kind=kOutput, calls=%fused_computation.10 | convolution fusion | flops 3288334336 | bytes 12386304 | tf_op jit(solution)/shard_map/dot_general | solution.py:21
  436.5 0.0 reduce-scatter.5.cloned.1.call-update
  436.6 0.0 copy-done.2
  436.6 0.6 dynamic-slice
  437.8 0.0 copy-start
  437.8 4.3 convert_reduce_fusion
  442.1 0.0 copy-done
  442.1 0.6 convert_reduce_fusion.1
  442.7 2.6 fusion.6
  445.3 12.2 %all-reduce = f32[448]{0:T(512)S(1)} all-reduce(f32[448]{0:T(512)S(1)} %bitcast.24), channel_id=4, replica_groups=mesh['dp'=2,'row'=4,'col'=4] {'col'}, use_global_device_ids=true, to_apply=%region_5.6.clone | all-reduce | flops 448 | bytes 3584
  457.5 0.1 dynamic-slice.1
  457.6 6.0 %psum.15 = f32[112]{0:T(128)S(1)} all-reduce(f32[112]{0:T(128)S(1)} %dynamic-slice.1), channel_id=1, replica_groups=mesh['dp'=2,'row'=4,'col'=4] {'row'}, use_global_device_ids=true, to_apply=%region_6.7 | all-reduce | flops 112 | bytes 896 | tf_op jit(solution)/shard_map/psum | solution.py:48
  463.6 5.1 %fusion.5 = f32[1,1024]{1,0:T(1,128)S(1)} fusion(f32[3584,1]{0,1:T(1,128)S(1)} %reshape.7, bf16[3584,1024]{1,0:T(8,128)(2,1)} %all-gather.8.cloned.1.call-done), kind=kOutput, calls=%fused_computation.11 | convolution fusion | flops 44040192 | bytes 7358464 | tf_op jit(solution)/shard_map/dot_general | solution.py:22
  468.8 18.3 %psum.14 = f32[1024]{0:T(1024)S(1)} all-reduce(f32[1024]{0:T(1024)S(1)} %bitcast.23), channel_id=1, replica_groups=mesh['dp'=2,'row'=4,'col'=4] {'dp','col'}, use_global_device_ids=true, to_apply=%region_3.4 | all-reduce | flops 1024 | bytes 8192 | tf_op jit(solution)/shard_map/psum | solution.py:47
  487.1 0.5 broadcast_multiply_fusion.1
  487.6 0.6 broadcast_multiply_fusion
  488.2 0.0 reduce-scatter.5.cloned.1.call-done
  488.2 1.7 convert_element_type.13
  (2 shorter events, 0.0 us)
Async XLA Ops:
  7.2 180.6 %all-gather.4.cloned.1.call-start = ((), (), s32[]{:S(2)}) async-start(), calls=%async_computation.2 | async-start | bytes 22020096 | tf_op jit(solution)/shard_map/all_gather | solution.py:36
  7.2 0.9 copy-start.1
  7.9 295.7 %reduce-scatter.3.cloned.1.call-start = ((), (), s32[]{:S(2)}) async-start(), calls=%async_computation.3 | async-start | bytes 16056320 | tf_op jit(solution)/shard_map/reduce_scatter | solution.py:14
  202.7 194.7 %all-gather.8.cloned.1.call-start = ((), (), s32[]{:S(2)}) async-start(), calls=%async_computation.5 | async-start | bytes 11010048 | tf_op jit(solution)/shard_map/all_gather | solution.py:41
  203.5 224.3 %all-gather.6.cloned.1.call-start = ((), (), s32[]{:S(2)}) async-start(), calls=%async_computation.4 | async-start | bytes 4014080 | tf_op jit(solution)/shard_map/all_gather | solution.py:15
  306.9 129.7 %copy-start.2 = (u32[32]{0:T(128)S(1)}, u32[32]{0:T(128)}, u32[]{:S(2)}) copy-start(u32[32]{0:T(128)} %constant.13) | copy-start | bytes 388
  306.9 181.3 %reduce-scatter.5.cloned.1.call-start = ((), (), s32[]{:S(2)}) async-start(), calls=%async_computation.6 | async-start | bytes 2293760 | tf_op jit(solution)/shard_map/reduce_scatter | solution.py:44
  437.8 4.3 copy-start
Sparse Core Ops, SparseCore 0:
  9.6 178.2 all-gather.3
  202.8 100.7 reduce-scatter.2
  305.2 92.1 all-gather.7
  398.8 28.9 all-gather.5
  436.7 39.7 reduce-scatter.4
where the time goes:
time: 497 us; the launch traced here: 496 us
  waiting for transfers between devices  379 us (76%)
  blocking collectives  59.3 us (12%)
  matrix products  31.4 us (6%)
  between operations  14.5 us (3%)
  other arithmetic  10.9 us (2%)
    all_gather x1, waiting for transfers between devices, per_device(): lax.all_gather(gate_up, 'dp', axis=2, tiled=True)  157 us
    reduce_scatter x1, waiting for transfers between devices, hidden_units(): lax.psum_scatter(partial_value, 'row', scatter_dimension=0, tiled=True)  100 us
    all_gather x1, waiting for transfers between devices, per_device(): lax.all_gather(down_weight, 'dp', axis=0, tiled=True)  90.5 us
    all_gather x1, waiting for transfers between devices, hidden_units(): return lax.all_gather(swiglu(share), 'row', axis=0, tiled=True)  30.4 us
    all_gather x1, blocking collectives, per_device(): group_rows = lax.all_gather(tokens, 'col', axis=0, tiled=True)  22.7 us
    psum x1, blocking collectives, per_device(): col_check = lax.psum(column_part, ('dp', 'col')) / math.sqrt(total_tokens)  18.3 us
    dot_general x1, matrix products, per_device(): jnp.einsum('td,gdf->tgf', group_rows, lax.all_gather(gate_up, 'dp', axis=...  14.9 us
    unnamed x1, blocking collectives  12.2 us
  transfers between devices with their start and end apart: 5, of which 4 were waited for; matrix products, arithmetic and copies ran while one was open for 4% of the time, Pallas kernels for 0%

commit v1 on v0

--- a/solution.py
+++ b/solution.py
@@ -1,9 +1,15 @@
+import functools
 import math
 
 import jax
 import jax.numpy as jnp
 from jax import lax
+from jax.experimental import pallas as pl
+from jax.experimental.pallas import tpu as pltpu
 from jax.sharding import PartitionSpec as P
+
+MESH = pl.DeviceIdType.MESH
+TILE = 256
 
 
 def swiglu(partial_value):
@@ -49,10 +55,396 @@
     return (mixed.astype(jnp.bfloat16), col_check, row_check)
 
 
+def dot(a, b):
+    return jnp.dot(a, b, preferred_element_type=jnp.float32)
+
+
+def dot_rows(a, b):
+    return lax.dot_general(a, b, (((1,), (1,)), ((), ())), preferred_element_type=jnp.float32)
+
+
+def three_terms(row):
+    high = row.astype(jnp.bfloat16)
+    rest = row - high.astype(jnp.float32)
+    middle = rest.astype(jnp.bfloat16)
+    low = (rest - middle.astype(jnp.float32)).astype(jnp.bfloat16)
+    index = lax.broadcasted_iota(jnp.int32, row.shape, 0)
+    terms = jnp.where(
+        index == 0,
+        high.astype(jnp.float32),
+        jnp.where(
+            index == 1,
+            middle.astype(jnp.float32),
+            jnp.where(index == 2, low.astype(jnp.float32), 0.0),
+        ),
+    )
+    return terms.astype(jnp.bfloat16)
+
+
+def kernel(
+    total_tokens,
+    model_width,
+    tokens_ref,
+    gate_up_ref,
+    down_ref,
+    mixed_ref,
+    col_ref,
+    row_ref,
+    weights,
+    down,
+    acts,
+    part_wide,
+    part_send,
+    part_recv,
+    hidden,
+    out_wide,
+    out_send,
+    x_recv,
+    z_send,
+    z_recv,
+    own_sum,
+    unit_sums,
+    weight_parts,
+    weight_terms,
+    small_send,
+    small_recv,
+    local_sem,
+    w_send,
+    w_recv,
+    tz_send,
+    tz_recv,
+    tx_send,
+    tx_recv,
+    tp_send,
+    tp_recv,
+    py_send,
+    py_recv,
+    hp_send,
+    hp_recv,
+    hy_send,
+    hy_recv,
+    hf_send,
+    hf_recv,
+    mx_send,
+    mx_recv,
+    mz_send,
+    mz_recv,
+    ws_send,
+    ws_recv,
+    sm_send,
+    sm_recv,
+):
+    block, width = tokens_ref.shape
+    units = down_ref.shape[0]
+    half = units // 2
+    x = lax.axis_index("dp")
+    row = lax.axis_index("row")
+    z = lax.axis_index("col")
+    y, core = lax.div(row, 2), lax.rem(row, 2)
+    nx, ny, ncore = 1 - x, 1 - y, 1 - core
+    zs = [z, z + 1 - 2 * lax.rem(z, 2), lax.rem(z + 2, 4), 3 - z]
+    partner = (x, y * 2 + ncore, z)
+    across_y = (x, ny * 2 + core, z)
+    across_x = (nx, row, z)
+    rows = [(x, lax.rem(row + k, 4), z) for k in range(1, 4)]
+    peers = [(x, row, zs[j]) for j in range(1, 4)] + [(nx, row, zs[j]) for j in range(4)]
+    small_slots = [(j, x) for j in range(1, 4)] + [(j, nx) for j in range(4)]
+    sent = []
+
+    def send(src, dst, send_sem, recv_sem, device):
+        copy = pltpu.make_async_remote_copy(
+            src_ref=src,
+            dst_ref=dst,
+            send_sem=send_sem,
+            recv_sem=recv_sem,
+            device_id=device,
+            device_id_type=MESH,
+        )
+        copy.start()
+        sent.append(copy)
+        return copy
+
+    def lanes(which):
+        return pl.ds(pl.multiple_of(which * half, 128), half)
+
+    local = [
+        pltpu.make_async_copy(tokens_ref, acts.at[z, core, x], local_sem.at[0]),
+        pltpu.make_async_copy(
+            gate_up_ref.at[0, :, lanes(core)], weights.at[core, :, 0:half], local_sem.at[1]
+        ),
+        pltpu.make_async_copy(
+            gate_up_ref.at[1, :, lanes(core)], weights.at[core, :, half:units], local_sem.at[2]
+        ),
+        pltpu.make_async_copy(down_ref, down, local_sem.at[3]),
+    ]
+    for copy in local:
+        copy.start()
+
+    barrier = pltpu.get_barrier_semaphore()
+    for device in rows + peers:
+        pl.semaphore_signal(barrier, inc=1, device_id=device, device_id_type=MESH)
+    pl.semaphore_wait(barrier, len(rows) + len(peers))
+
+    tx, tp, tz = {}, {}, {}
+    tx[0] = send(tokens_ref, acts.at[z, core, x], tx_send.at[0], tx_recv.at[0], across_x)
+    tp[0, 0] = send(tokens_ref, acts.at[z, core, x], tp_send.at[0], tp_recv.at[0], partner)
+    for j in range(1, 4):
+        tz[j] = send(
+            tokens_ref, acts.at[z, core, x], tz_send.at[j - 1], tz_recv.at[j - 1], peers[j - 1]
+        )
+    swap = [
+        send(
+            gate_up_ref.at[g, :, lanes(ncore)],
+            weights.at[core, :, g * half : (g + 1) * half],
+            w_send.at[g],
+            w_recv.at[g],
+            partner,
+        )
+        for g in range(2)
+    ]
+
+    unit_sums[...] = jnp.zeros_like(unit_sums)
+    small_send[...] = jnp.zeros_like(small_send)
+
+    local[3].wait()
+    ones_width = jnp.ones((8, width), jnp.bfloat16)
+    for h in range(2):
+        weight_parts[row, h] = dot_rows(ones_width, down[h * half : (h + 1) * half, :])
+    weight_copies = [
+        send(
+            weight_parts.at[row], weight_parts.at[row], ws_send.at[k], ws_recv.at[k], rows[k]
+        )
+        for k in range(3)
+    ]
+
+    def arrive(j):
+        tz[j].wait_recv()
+        place = acts.at[zs[j], core, x]
+        tx[j] = send(place, place, tx_send.at[j], tx_recv.at[j], across_x)
+        tp[j, 0] = send(place, place, tp_send.at[2 * j], tp_recv.at[2 * j], partner)
+
+    def arrive_across(j):
+        tx[j].wait_recv()
+        place = acts.at[zs[j], core, nx]
+        tp[j, 1] = send(place, place, tp_send.at[2 * j + 1], tp_recv.at[2 * j + 1], partner)
+
+    py, hp, hy, hf, mx, mz = {}, {}, {}, {}, {}, {}
+
+    def gate_and_up(j):
+        tp[j, 0].wait_recv()
+        tp[j, 1].wait_recv()
+
+        def body(t, carry):
+            columns = pl.ds(pl.multiple_of(t * TILE, TILE), TILE)
+            product = dot(
+                acts[zs[j], 0].reshape(2 * block, width), weights[0, :, columns]
+            ) + dot(acts[zs[j], 1].reshape(2 * block, width), weights[1, :, columns])
+            product = product.reshape(2, block, TILE)
+            part_wide[j, :, :, columns] = product
+            part_send[j, :, :, columns] = product.astype(jnp.bfloat16)
+            return carry
+
+        lax.fori_loop(0, units // TILE, body, 0)
+        py[j] = send(
+            part_send.at[j, ny], part_recv.at[j], py_send.at[j], py_recv.at[j], across_y
+        )
+
+    def activate(j):
+        py[j].wait_recv()
+        gate = part_wide[j, y, :, 0:half] + part_recv[j, :, 0:half].astype(jnp.float32)
+        up = part_wide[j, y, :, half:units] + part_recv[j, :, half:units].astype(jnp.float32)
+        hidden[j, core, y] = (gate / (1.0 + jnp.exp(-gate)) * up).astype(jnp.bfloat16)
+        place = hidden.at[j, core, y]
+        hy[j] = send(place, place, hy_send.at[j], hy_recv.at[j], across_y)
+        hp[j] = send(place, place, hp_send.at[j], hp_recv.at[j], partner)
+
+    def hand_over(j):
+        hy[j].wait_recv()
+        place = hidden.at[j, core, ny]
+        hf[j] = send(place, place, hf_send.at[j], hf_recv.at[j], partner)
+
+    def down_part(j):
+        hp[j].wait_recv()
+        hf[j].wait_recv()
+
+        def body(t, carry):
+            columns = pl.ds(pl.multiple_of(t * TILE, TILE), TILE)
+            product = dot(
+                hidden[j, 0].reshape(2 * block, half), down[0:half, columns]
+            ) + dot(hidden[j, 1].reshape(2 * block, half), down[half:units, columns])
+            product = product.reshape(2, block, TILE)
+            out_wide[j, :, :, columns] = product
+            out_send[j, :, :, columns] = product.astype(jnp.bfloat16)
+            return carry
+
+        lax.fori_loop(0, width // TILE, body, 0)
+        mx[j] = send(out_send.at[j, nx], x_recv.at[j], mx_send.at[j], mx_recv.at[j], across_x)
+
+    def checks(j):
+        ones = jnp.ones((8, 2 * block), jnp.bfloat16)
+        for h in range(2):
+            unit_sums[h] += dot(ones, hidden[j, h].reshape(2 * block, half))
+        for b in range(2):
+            terms = dot_rows(weight_terms[0], hidden[j, 0, b]) + dot_rows(
+                weight_terms[1], hidden[j, 1, b]
+            )
+            small_send[j, b, 8:9, 0:block] = jnp.sum(terms, axis=0, keepdims=True)
+
+    def add_across(j):
+        mx[j].wait_recv()
+        value = out_wide[j, x] + x_recv[j].astype(jnp.float32)
+        if j == 0:
+            own_sum[...] = value
+        else:
+            z_send[j - 1] = value.astype(jnp.bfloat16)
+            mz[j] = send(
+                z_send.at[j - 1],
+                z_recv.at[j - 1],
+                mz_send.at[j - 1],
+                mz_recv.at[j - 1],
+                peers[j - 1],
+            )
+
+    arrive_across(0)
+    arrive(1)
+    for copy in local[:3]:
+        copy.wait()
+    for copy in swap:
+        copy.wait_recv()
+    gate_and_up(0)
+    arrive_across(1)
+    arrive(2)
+    gate_and_up(1)
+    for copy in weight_copies:
+        copy.wait_recv()
+    for h in range(2):
+        weight_terms[h] = three_terms(
+            weight_parts[0, h] + weight_parts[1, h] + weight_parts[2, h] + weight_parts[3, h]
+        )
+    activate(0)
+    arrive_across(2)
+    arrive(3)
+    gate_and_up(2)
+    activate(1)
+    hand_over(0)
+    arrive_across(3)
+    gate_and_up(3)
+    hand_over(1)
+    down_part(0)
+    activate(2)
+    down_part(1)
+    add_across(0)
+    checks(0)
+    hand_over(2)
+    activate(3)
+    add_across(1)
+    down_part(2)
+    checks(1)
+    checks(2)
+    hand_over(3)
+    add_across(2)
+    down_part(3)
+    checks(3)
+
+    column_terms = dot(three_terms(unit_sums[0]), down[0:half, :]) + dot(
+        three_terms(unit_sums[1]), down[half:units, :]
+    )
+    columns = jnp.sum(column_terms, axis=0, keepdims=True)
+    for j in range(4):
+        for b in range(2):
+            for k in range(width // 128):
+                small_send[j, b, k : k + 1, :] = columns[:, k * 128 : (k + 1) * 128]
+    me = x * 4 + z
+    small_recv[me] = small_send[0, x]
+    small = [
+        send(
+            small_send.at[slot[0], slot[1]],
+            small_recv.at[me],
+            sm_send.at[k],
+            sm_recv.at[k],
+            peers[k],
+        )
+        for k, slot in enumerate(small_slots)
+    ]
+    add_across(3)
+    for copy in small:
+        copy.wait_recv()
+    total = small_recv[0]
+    for k in range(1, 8):
+        total = total + small_recv[k]
+    col_ref[...] = total[0:8] / math.sqrt(total_tokens)
+    row_ref[...] = total[8:16] / math.sqrt(model_width)
+    for j in range(1, 4):
+        mz[j].wait_recv()
+    mixed_ref[...] = (
+        own_sum[...]
+        + z_recv[0].astype(jnp.float32)
+        + z_recv[1].astype(jnp.float32)
+        + z_recv[2].astype(jnp.float32)
+    ).astype(jnp.bfloat16)
+    for copy in sent:
+        copy.wait_send()
+
+
+def per_device_kernel(tokens, gate_up, down_weight):
+    block, width = tokens.shape
+    units = down_weight.shape[0]
+    half = units // 2
+    total_tokens = block * lax.axis_size(("dp", "col"))
+    model_width = width * lax.axis_size("row")
+    dma = pltpu.SemaphoreType.DMA
+    bf16, f32 = jnp.bfloat16, jnp.float32
+    sems = []
+    for count in (2, 3, 4, 8, 4, 4, 4, 4, 4, 3, 3, 7):
+        sems += [dma((count,)), dma((count,))]
+    mixed, col, row = pl.pallas_call(
+        functools.partial(kernel, total_tokens, model_width),
+        out_shape=(
+            jax.ShapeDtypeStruct((block, width), bf16),
+            jax.ShapeDtypeStruct((8, 128), f32),
+            jax.ShapeDtypeStruct((8, 128), f32),
+        ),
+        in_specs=[pl.BlockSpec(memory_space=pl.ANY)] * 3,
+        out_specs=(pl.BlockSpec(memory_space=pltpu.VMEM),) * 3,
+        scratch_shapes=[
+            pltpu.VMEM((2, width, units), bf16),
+            pltpu.VMEM((units, width), bf16),
+            pltpu.VMEM((4, 2, 2, block, width), bf16),
+            pltpu.VMEM((4, 2, block, units), f32),
+            pltpu.VMEM((4, 2, block, units), bf16),
+            pltpu.VMEM((4, block, units), bf16),
+            pltpu.VMEM((4, 2, 2, block, half), bf16),
+            pltpu.VMEM((4, 2, block, width), f32),
+            pltpu.VMEM((4, 2, block, width), bf16),
+            pltpu.VMEM((4, block, width), bf16),
+            pltpu.VMEM((3, block, width), bf16),
+            pltpu.VMEM((3, block, width), bf16),
+            pltpu.VMEM((block, width), f32),
+            pltpu.VMEM((2, 8, half), f32),
+            pltpu.VMEM((4, 2, 8, half), f32),
+            pltpu.VMEM((2, 8, half), bf16),
+            pltpu.VMEM((4, 2, 16, 128), f32),
+            pltpu.VMEM((8, 16, 128), f32),
+            dma((4,)),
+        ]
+        + sems,
+        compiler_params=pltpu.CompilerParams(
+            collective_id=0, has_side_effects=True, vmem_limit_bytes=56 * 2**20
+        ),
+        name="swiglu_grid",
+    )(tokens, gate_up, down_weight)
+    return mixed, col.reshape(width), row[0, :block]
+
+
+def fits_kernel(mesh):
+    return dict(mesh.shape) == {"dp": 2, "row": 4, "col": 4}
+
+
 def solution(mesh):
+    body = per_device_kernel if fits_kernel(mesh) else per_device
     placed = (P(("dp", "col"), "row"), P(None, "row", ("dp", "col")), P(("dp", "col"), "row"))
     return jax.shard_map(
-        per_device,
+        body,
         mesh=mesh,
         in_specs=placed,
         out_specs=(P(("dp", "col"), "row"), P("row"), P(("dp", "col"))),

time: 497 us -> 103 us (0.21)
  the two profiles are of different devices: /device:TPU:0 before, /device:TPU:16 now
where the time goes in v1:
time: 103 us
  Pallas kernels  98.4 us (96%)
  local copies, waits for them, and re-layouts  4.1 us (4%)
    pallas_call x1, Pallas kernels, per_device_kernel(): pl.pallas_call(functools.partial(kernel, total_tokens, model_width), out_...  98.4 us
    unnamed x2, local copies, waits for them, and re-layouts  2.91 us

profile of v1, /device:TPU:16, one launch (start us, length us, event | category | flops | bytes accessed | tf_op | source)
XLA Modules:
  0.0 103.2 jit_solution(3371957987950999191)
XLA Ops:
  0.6 98.4 %swiglu_grid.1 = (bf16[112,1024]{1,0:T(8,128)(2,1)}, f32[8,128]{1,0:T(8,128)}, f32[8,128]{1,0:T(8,128)}) custom-call(bf16[112,1024]{1,0:T(8,128)(2,1)} %tokens_ref.1, bf16[2,1024,1792]{2,1,0:T(8,128)(2,1)} %gate_up_ref.1, bf16[1792,1024]{1,0:T(8,128)(2,1)} %down_ref.1), custom_call_target="tpu_custom_call" | custom-call | tf_op jit(solution)/shard_map/swiglu_grid/pallas_call | solution.py:400
  99.1 1.2 %slice_bitcast_fusion = f32[112]{0:T(128)} fusion(f32[8,128]{1,0:T(8,128)} %get-tuple-element.8), kind=kLoop, calls=%fused_computation | loop fusion | bytes 896 | tf_op jit(solution)/shard_map/squeeze | solution.py:436
  100.3 1.6 %copy.8 = bf16[112,1024]{1,0:T(8,128)(2,1)} copy(bf16[112,1024]{1,0:T(8,128)(2,1)} %get-tuple-element.12) | data formatting | bytes 458752
  101.9 1.3 %copy.9 = f32[1024]{0:T(1024)} copy(f32[1024]{0:T(1024)} %bitcast.3) | data formatting | bytes 8192

commit v2 on v1

--- a/solution.py
+++ b/solution.py
@@ -137,12 +137,15 @@
     block, width = tokens_ref.shape
     units = down_ref.shape[0]
     half = units // 2
+    first = (half // 128 + 1) // 2 * 128
+    pieces = [(0, first, 0), (first, half - first, 2 * first)]
+    strip = width // 2
     x = lax.axis_index("dp")
     row = lax.axis_index("row")
     z = lax.axis_index("col")
     y, core = lax.div(row, 2), lax.rem(row, 2)
     nx, ny, ncore = 1 - x, 1 - y, 1 - core
-    zs = [z, z + 1 - 2 * lax.rem(z, 2), lax.rem(z + 2, 4), 3 - z]
+    zs = [z, lax.rem(z + 2, 4), 3 - z, z + 1 - 2 * lax.rem(z, 2)]
     partner = (x, y * 2 + ncore, z)
     across_y = (x, ny * 2 + core, z)
     across_x = (nx, row, z)
@@ -164,19 +167,17 @@
         sent.append(copy)
         return copy
 
-    def lanes(which):
-        return pl.ds(pl.multiple_of(which * half, 128), half)
-
-    local = [
-        pltpu.make_async_copy(tokens_ref, acts.at[z, core, x], local_sem.at[0]),
-        pltpu.make_async_copy(
-            gate_up_ref.at[0, :, lanes(core)], weights.at[core, :, 0:half], local_sem.at[1]
-        ),
-        pltpu.make_async_copy(
-            gate_up_ref.at[1, :, lanes(core)], weights.at[core, :, half:units], local_sem.at[2]
-        ),
-        pltpu.make_async_copy(down_ref, down, local_sem.at[3]),
-    ]
+    def weight_slices(which):
+        for start, count, column in pieces:
+            lanes = pl.ds(pl.multiple_of(which * half + start, 128), count)
+            for g in range(2):
+                place = slice(column + g * count, column + (g + 1) * count)
+                yield gate_up_ref.at[g, :, lanes], weights.at[core, :, place]
+
+    local = [pltpu.make_async_copy(tokens_ref, acts.at[z, core, x], local_sem.at[0])]
+    for k, (src, dst) in enumerate(weight_slices(core)):
+        local.append(pltpu.make_async_copy(src, dst, local_sem.at[1 + k]))
+    local.append(pltpu.make_async_copy(down_ref, down, local_sem.at[5]))
     for copy in local:
         copy.start()
 
@@ -188,34 +189,39 @@
     tx, tp, tz = {}, {}, {}
     tx[0] = send(tokens_ref, acts.at[z, core, x], tx_send.at[0], tx_recv.at[0], across_x)
     tp[0, 0] = send(tokens_ref, acts.at[z, core, x], tp_send.at[0], tp_recv.at[0], partner)
-    for j in range(1, 4):
+
+    def offer(j):
         tz[j] = send(
             tokens_ref, acts.at[z, core, x], tz_send.at[j - 1], tz_recv.at[j - 1], peers[j - 1]
         )
+
+    offer(1)
     swap = [
-        send(
-            gate_up_ref.at[g, :, lanes(ncore)],
-            weights.at[core, :, g * half : (g + 1) * half],
-            w_send.at[g],
-            w_recv.at[g],
-            partner,
-        )
-        for g in range(2)
+        send(src, dst, w_send.at[k], w_recv.at[k], partner)
+        for k, (src, dst) in enumerate(weight_slices(ncore))
     ]
 
     unit_sums[...] = jnp.zeros_like(unit_sums)
     small_send[...] = jnp.zeros_like(small_send)
 
-    local[3].wait()
-    ones_width = jnp.ones((8, width), jnp.bfloat16)
-    for h in range(2):
-        weight_parts[row, h] = dot_rows(ones_width, down[h * half : (h + 1) * half, :])
-    weight_copies = [
-        send(
-            weight_parts.at[row], weight_parts.at[row], ws_send.at[k], ws_recv.at[k], rows[k]
-        )
-        for k in range(3)
-    ]
+    weight_copies = []
+
+    def sum_weights():
+        local[5].wait()
+        ones_width = jnp.ones((8, width), jnp.bfloat16)
+        for h in range(2):
+            weight_parts[row, h] = dot_rows(ones_width, down[h * half : (h + 1) * half, :])
+        place = weight_parts.at[row]
+        for k in range(3):
+            weight_copies.append(send(place, place, ws_send.at[k], ws_recv.at[k], rows[k]))
+
+    def total_weights():
+        for copy in weight_copies:
+            copy.wait_recv()
+        for h in range(2):
+            weight_terms[h] = three_terms(
+                weight_parts[0, h] + weight_parts[1, h] + weight_parts[2, h] + weight_parts[3, h]
+            )
 
     def arrive(j):
         tz[j].wait_recv()
@@ -230,9 +236,12 @@
 
     py, hp, hy, hf, mx, mz = {}, {}, {}, {}, {}, {}
 
-    def gate_and_up(j):
+    def ready(j):
         tp[j, 0].wait_recv()
         tp[j, 1].wait_recv()
+
+    def gate_and_up(j, p):
+        _, count, column = pieces[p]
 
         def body(t, carry):
             columns = pl.ds(pl.multiple_of(t * TILE, TILE), TILE)
@@ -244,28 +253,44 @@
             part_send[j, :, :, columns] = product.astype(jnp.bfloat16)
             return carry
 
-        lax.fori_loop(0, units // TILE, body, 0)
-        py[j] = send(
-            part_send.at[j, ny], part_recv.at[j], py_send.at[j], py_recv.at[j], across_y
+        lax.fori_loop(column // TILE, (column + 2 * count) // TILE, body, 0)
+        place = slice(column, column + 2 * count)
+        py[j, p] = send(
+            part_send.at[j, ny, :, place],
+            part_recv.at[j, :, place],
+            py_send.at[2 * j + p],
+            py_recv.at[2 * j + p],
+            across_y,
         )
 
-    def activate(j):
-        py[j].wait_recv()
-        gate = part_wide[j, y, :, 0:half] + part_recv[j, :, 0:half].astype(jnp.float32)
-        up = part_wide[j, y, :, half:units] + part_recv[j, :, half:units].astype(jnp.float32)
-        hidden[j, core, y] = (gate / (1.0 + jnp.exp(-gate)) * up).astype(jnp.bfloat16)
-        place = hidden.at[j, core, y]
-        hy[j] = send(place, place, hy_send.at[j], hy_recv.at[j], across_y)
-        hp[j] = send(place, place, hp_send.at[j], hp_recv.at[j], partner)
-
-    def hand_over(j):
-        hy[j].wait_recv()
-        place = hidden.at[j, core, ny]
-        hf[j] = send(place, place, hf_send.at[j], hf_recv.at[j], partner)
+    def activate(j, p):
+        start, count, column = pieces[p]
+        py[j, p].wait_recv()
+        gate, up = [
+            part_wide[j, y, :, place] + part_recv[j, :, place].astype(jnp.float32)
+            for place in (
+                slice(column, column + count),
+                slice(column + count, column + 2 * count),
+            )
+        ]
+        lanes = slice(start, start + count)
+        hidden[j, core, y, :, lanes] = (gate / (1.0 + jnp.exp(-gate)) * up).astype(jnp.bfloat16)
+        place = hidden.at[j, core, y, :, lanes]
+        n = 2 * j + p
+        hy[j, p] = send(place, place, hy_send.at[n], hy_recv.at[n], across_y)
+        hp[j, p] = send(place, place, hp_send.at[n], hp_recv.at[n], partner)
+
+    def hand_over(j, p):
+        start, count, _ = pieces[p]
+        hy[j, p].wait_recv()
+        place = hidden.at[j, core, ny, :, start : start + count]
+        n = 2 * j + p
+        hf[j, p] = send(place, place, hf_send.at[n], hf_recv.at[n], partner)
 
     def down_part(j):
-        hp[j].wait_recv()
-        hf[j].wait_recv()
+        for p in range(2):
+            hp[j, p].wait_recv()
+            hf[j, p].wait_recv()
 
         def body(t, carry):
             columns = pl.ds(pl.multiple_of(t * TILE, TILE), TILE)
@@ -277,8 +302,17 @@
             out_send[j, :, :, columns] = product.astype(jnp.bfloat16)
             return carry
 
-        lax.fori_loop(0, width // TILE, body, 0)
-        mx[j] = send(out_send.at[j, nx], x_recv.at[j], mx_send.at[j], mx_recv.at[j], across_x)
+        for q in range(2):
+            lax.fori_loop(q * strip // TILE, (q + 1) * strip // TILE, body, 0)
+            place = slice(q * strip, (q + 1) * strip)
+            n = 2 * j + q
+            mx[j, q] = send(
+                out_send.at[j, nx, :, place],
+                x_recv.at[j, :, place],
+                mx_send.at[n],
+                mx_recv.at[n],
+                across_x,
+            )
 
     def checks(j):
         ones = jnp.ones((8, 2 * block), jnp.bfloat16)
@@ -291,58 +325,79 @@
             small_send[j, b, 8:9, 0:block] = jnp.sum(terms, axis=0, keepdims=True)
 
     def add_across(j):
-        mx[j].wait_recv()
-        value = out_wide[j, x] + x_recv[j].astype(jnp.float32)
-        if j == 0:
-            own_sum[...] = value
-        else:
-            z_send[j - 1] = value.astype(jnp.bfloat16)
-            mz[j] = send(
-                z_send.at[j - 1],
-                z_recv.at[j - 1],
-                mz_send.at[j - 1],
-                mz_recv.at[j - 1],
-                peers[j - 1],
-            )
-
+        for q in range(2):
+            mx[j, q].wait_recv()
+            place = slice(q * strip, (q + 1) * strip)
+            value = out_wide[j, x, :, place] + x_recv[j, :, place].astype(jnp.float32)
+            if j == 0:
+                own_sum[:, place] = value
+            else:
+                z_send[j - 1, :, place] = value.astype(jnp.bfloat16)
+                n = 2 * (j - 1) + q
+                mz[j, q] = send(
+                    z_send.at[j - 1, :, place],
+                    z_recv.at[j - 1, :, place],
+                    mz_send.at[n],
+                    mz_recv.at[n],
+                    peers[j - 1],
+                )
+
+    def weights_here(p):
+        for k in (2 * p, 2 * p + 1):
+            local[1 + k].wait()
+            swap[k].wait_recv()
+
+    local[0].wait()
     arrive_across(0)
+    weights_here(0)
+    ready(0)
+    gate_and_up(0, 0)
+    weights_here(1)
+    gate_and_up(0, 1)
     arrive(1)
-    for copy in local[:3]:
-        copy.wait()
-    for copy in swap:
-        copy.wait_recv()
-    gate_and_up(0)
+    offer(2)
+    sum_weights()
+    activate(0, 0)
     arrive_across(1)
+    ready(1)
+    gate_and_up(1, 0)
+    gate_and_up(1, 1)
     arrive(2)
-    gate_and_up(1)
-    for copy in weight_copies:
-        copy.wait_recv()
-    for h in range(2):
-        weight_terms[h] = three_terms(
-            weight_parts[0, h] + weight_parts[1, h] + weight_parts[2, h] + weight_parts[3, h]
-        )
-    activate(0)
+    offer(3)
+    activate(0, 1)
+    hand_over(0, 0)
+    total_weights()
     arrive_across(2)
+    ready(2)
+    gate_and_up(2, 0)
+    gate_and_up(2, 1)
     arrive(3)
-    gate_and_up(2)
-    activate(1)
-    hand_over(0)
+    activate(1, 0)
+    hand_over(0, 1)
+    activate(1, 1)
     arrive_across(3)
-    gate_and_up(3)
-    hand_over(1)
+    ready(3)
+    gate_and_up(3, 0)
+    gate_and_up(3, 1)
+    hand_over(1, 0)
     down_part(0)
-    activate(2)
+    activate(2, 0)
+    hand_over(1, 1)
+    activate(2, 1)
     down_part(1)
     add_across(0)
     checks(0)
-    hand_over(2)
-    activate(3)
+    hand_over(2, 0)
+    activate(3, 0)
+    hand_over(2, 1)
+    activate(3, 1)
     add_across(1)
     down_part(2)
     checks(1)
     checks(2)
-    hand_over(3)
     add_across(2)
+    hand_over(3, 0)
+    hand_over(3, 1)
     down_part(3)
     checks(3)
 
@@ -374,14 +429,13 @@
         total = total + small_recv[k]
     col_ref[...] = total[0:8] / math.sqrt(total_tokens)
     row_ref[...] = total[8:16] / math.sqrt(model_width)
-    for j in range(1, 4):
-        mz[j].wait_recv()
-    mixed_ref[...] = (
-        own_sum[...]
-        + z_recv[0].astype(jnp.float32)
-        + z_recv[1].astype(jnp.float32)
-        + z_recv[2].astype(jnp.float32)
-    ).astype(jnp.bfloat16)
+    for q in range(2):
+        place = slice(q * strip, (q + 1) * strip)
+        value = own_sum[:, place]
+        for j in range(1, 4):
+            mz[j, q].wait_recv()
+            value = value + z_recv[j - 1, :, place].astype(jnp.float32)
+        mixed_ref[:, place] = value.astype(jnp.bfloat16)
     for copy in sent:
         copy.wait_send()
 
@@ -395,7 +449,7 @@
     dma = pltpu.SemaphoreType.DMA
     bf16, f32 = jnp.bfloat16, jnp.float32
     sems = []
-    for count in (2, 3, 4, 8, 4, 4, 4, 4, 4, 3, 3, 7):
+    for count in (4, 3, 4, 8, 8, 8, 8, 8, 8, 6, 3, 7):
         sems += [dma((count,)), dma((count,))]
     mixed, col, row = pl.pallas_call(
         functools.partial(kernel, total_tokens, model_width),
@@ -425,7 +479,7 @@
             pltpu.VMEM((2, 8, half), bf16),
             pltpu.VMEM((4, 2, 16, 128), f32),
             pltpu.VMEM((8, 16, 128), f32),
-            dma((4,)),
+            dma((6,)),
         ]
         + sems,
         compiler_params=pltpu.CompilerParams(

time: 103 us -> 97.2 us (0.944)
  the two profiles are of different devices: /device:TPU:16 before, /device:TPU:0 now
where the time goes in v2:
time: 97.2 us; the launch traced here: 97 us
  Pallas kernels  92.2 us (95%)
  local copies, waits for them, and re-layouts  4.1 us (4%)
    pallas_call x1, Pallas kernels, per_device_kernel(): pl.pallas_call(functools.partial(kernel, total_tokens, model_width), out_...  92.2 us
    unnamed x2, local copies, waits for them, and re-layouts  2.91 us

profile of v2, /device:TPU:0, one launch (start us, length us, event | category | flops | bytes accessed | tf_op | source)
XLA Modules:
  0.0 97.0 jit_solution(7639609609580352067)
XLA Ops:
  0.6 92.2 %swiglu_grid.1 = (bf16[112,1024]{1,0:T(8,128)(2,1)}, f32[8,128]{1,0:T(8,128)}, f32[8,128]{1,0:T(8,128)}) custom-call(bf16[112,1024]{1,0:T(8,128)(2,1)} %tokens_ref.1, bf16[2,1024,1792]{2,1,0:T(8,128)(2,1)} %gate_up_ref.1, bf16[1792,1024]{1,0:T(8,128)(2,1)} %down_ref.1), custom_call_target="tpu_custom_call" | custom-call | tf_op jit(solution)/shard_map/swiglu_grid/pallas_call | solution.py:454
  92.9 1.2 %slice_bitcast_fusion = f32[112]{0:T(128)} fusion(f32[8,128]{1,0:T(8,128)} %get-tuple-element.8), kind=kLoop, calls=%fused_computation | loop fusion | bytes 896 | tf_op jit(solution)/shard_map/squeeze | solution.py:490
  94.1 1.6 %copy.8 = bf16[112,1024]{1,0:T(8,128)(2,1)} copy(bf16[112,1024]{1,0:T(8,128)(2,1)} %get-tuple-element.12) | data formatting | bytes 458752
  95.7 1.3 %copy.9 = f32[1024]{0:T(1024)} copy(f32[1024]{0:T(1024)} %bitcast.3) | data formatting | bytes 8192

commit v3 on v2

--- a/solution.py
+++ b/solution.py
@@ -137,15 +137,16 @@
     block, width = tokens_ref.shape
     units = down_ref.shape[0]
     half = units // 2
-    first = (half // 128 + 1) // 2 * 128
-    pieces = [(0, first, 0), (first, half - first, 2 * first)]
+    group = half // 256 * 128
+    left = half - 2 * group
+    wide, last = 2 * group, 4 * group
     strip = width // 2
     x = lax.axis_index("dp")
     row = lax.axis_index("row")
     z = lax.axis_index("col")
     y, core = lax.div(row, 2), lax.rem(row, 2)
     nx, ny, ncore = 1 - x, 1 - y, 1 - core
-    zs = [z, lax.rem(z + 2, 4), 3 - z, z + 1 - 2 * lax.rem(z, 2)]
+    zs = [z, z + 1 - 2 * lax.rem(z, 2), lax.rem(z + 2, 4), 3 - z]
     partner = (x, y * 2 + ncore, z)
     across_y = (x, ny * 2 + core, z)
     across_x = (nx, row, z)
@@ -168,16 +169,16 @@
         return copy
 
     def weight_slices(which):
-        for start, count, column in pieces:
-            lanes = pl.ds(pl.multiple_of(which * half + start, 128), count)
+        for start, count in ((ny * group, group), (2 * group, left), (y * group, group)):
             for g in range(2):
-                place = slice(column + g * count, column + (g + 1) * count)
+                lanes = pl.ds(pl.multiple_of(which * half + start, 128), count)
+                place = pl.ds(pl.multiple_of(2 * start + g * count, 128), count)
                 yield gate_up_ref.at[g, :, lanes], weights.at[core, :, place]
 
     local = [pltpu.make_async_copy(tokens_ref, acts.at[z, core, x], local_sem.at[0])]
     for k, (src, dst) in enumerate(weight_slices(core)):
         local.append(pltpu.make_async_copy(src, dst, local_sem.at[1 + k]))
-    local.append(pltpu.make_async_copy(down_ref, down, local_sem.at[5]))
+    local.append(pltpu.make_async_copy(down_ref, down, local_sem.at[7]))
     for copy in local:
         copy.start()
 
@@ -207,7 +208,7 @@
     weight_copies = []
 
     def sum_weights():
-        local[5].wait()
+        local[7].wait()
         ones_width = jnp.ones((8, width), jnp.bfloat16)
         for h in range(2):
             weight_parts[row, h] = dot_rows(ones_width, down[h * half : (h + 1) * half, :])
@@ -240,11 +241,23 @@
         tp[j, 0].wait_recv()
         tp[j, 1].wait_recv()
 
-    def gate_and_up(j, p):
-        _, count, column = pieces[p]
-
+    def columns_of(tile):
+        return pl.ds(pl.multiple_of(tile * TILE, TILE), TILE)
+
+    def multiply_block(b, tile, tiles):
         def body(t, carry):
-            columns = pl.ds(pl.multiple_of(t * TILE, TILE), TILE)
+            columns = columns_of(tile + t)
+            product = dot(acts[z, 0, b], weights[0, :, columns]) + dot(
+                acts[z, 1, b], weights[1, :, columns]
+            )
+            part_send[0, b, :, columns] = product.astype(jnp.bfloat16)
+            return carry
+
+        lax.fori_loop(0, tiles, body, 0)
+
+    def multiply(j, tile, tiles):
+        def body(t, carry):
+            columns = columns_of(tile + t)
             product = dot(
                 acts[zs[j], 0].reshape(2 * block, width), weights[0, :, columns]
             ) + dot(acts[zs[j], 1].reshape(2 * block, width), weights[1, :, columns])
@@ -253,47 +266,75 @@
             part_send[j, :, :, columns] = product.astype(jnp.bfloat16)
             return carry
 
-        lax.fori_loop(column // TILE, (column + 2 * count) // TILE, body, 0)
-        place = slice(column, column + 2 * count)
-        py[j, p] = send(
-            part_send.at[j, ny, :, place],
-            part_recv.at[j, :, place],
-            py_send.at[2 * j + p],
-            py_recv.at[2 * j + p],
+        lax.fori_loop(0, tiles, body, 0)
+
+    def send_part(n, j, b, place):
+        py[n] = send(
+            part_send.at[j, b, :, place],
+            part_recv.at[j, b, :, place],
+            py_send.at[n],
+            py_recv.at[n],
             across_y,
         )
 
-    def activate(j, p):
-        start, count, column = pieces[p]
-        py[j, p].wait_recv()
-        gate, up = [
-            part_wide[j, y, :, place] + part_recv[j, :, place].astype(jnp.float32)
-            for place in (
-                slice(column, column + count),
-                slice(column + count, column + 2 * count),
-            )
-        ]
-        lanes = slice(start, start + count)
-        hidden[j, core, y, :, lanes] = (gate / (1.0 + jnp.exp(-gate)) * up).astype(jnp.bfloat16)
-        place = hidden.at[j, core, y, :, lanes]
-        n = 2 * j + p
-        hy[j, p] = send(place, place, hy_send.at[n], hy_recv.at[n], across_y)
-        hp[j, p] = send(place, place, hp_send.at[n], hp_recv.at[n], partner)
-
-    def hand_over(j, p):
-        start, count, _ = pieces[p]
-        hy[j, p].wait_recv()
-        place = hidden.at[j, core, ny, :, start : start + count]
-        n = 2 * j + p
-        hf[j, p] = send(place, place, hf_send.at[n], hf_recv.at[n], partner)
+    def at_128(start, count):
+        return pl.ds(pl.multiple_of(start, 128), count)
+
+    def terms_of(n):
+        if n < 2:
+            return 0, [((x, nx)[n], y * wide, group, y * group)]
+        if n == 2:
+            return 0, [(y, last, left, wide)]
+        j, p = divmod(n - 1, 2)
+        if p == 0:
+            return j, [(y, 0, group, 0)]
+        return j, [(y, wide, group, group), (y, last, left, wide)]
+
+    def hidden_place(n, who):
+        if n < 2:
+            return hidden.at[0, core, (x, nx)[n], :, at_128(who * group, group)]
+        if n == 2:
+            return hidden.at[0, core, who, :, wide:half]
+        j, p = divmod(n - 1, 2)
+        lanes = slice(0, group) if p == 0 else slice(group, half)
+        return hidden.at[j, core, who, :, lanes]
+
+    def activate(n):
+        py[n].wait_recv()
+        j, terms = terms_of(n)
+        for b, column, count, unit in terms:
+            gate, up = [
+                part_wide[j, b, :, place] + part_recv[j, b, :, place].astype(jnp.float32)
+                for place in (at_128(column, count), at_128(column + count, count))
+            ]
+            value = gate / (1.0 + jnp.exp(-gate)) * up
+            hidden[j, core, b, :, at_128(unit, count)] = value.astype(jnp.bfloat16)
+        place = hidden_place(n, y)
+        hp[n] = send(place, place, hp_send.at[n], hp_recv.at[n], partner)
+
+    def across(n):
+        place = hidden_place(n, y)
+        hy[n] = send(place, place, hy_send.at[n], hy_recv.at[n], across_y)
+
+    def hand_over(n):
+        hy[n].wait_recv()
+        place = hidden_place(n, ny)
+        hf[n] = send(place, place, hf_send.at[n], hf_recv.at[n], partner)
+
+    def gate_and_up(j):
+        ready(j)
+        multiply(j, 0, wide // TILE)
+        send_part(1 + 2 * j, j, ny, slice(0, wide))
+        multiply(j, wide // TILE, (units - wide) // TILE)
+        send_part(2 + 2 * j, j, ny, slice(wide, units))
 
     def down_part(j):
-        for p in range(2):
-            hp[j, p].wait_recv()
-            hf[j, p].wait_recv()
+        for n in (0, 1, 2) if j == 0 else (1 + 2 * j, 2 + 2 * j):
+            hp[n].wait_recv()
+            hf[n].wait_recv()
 
         def body(t, carry):
-            columns = pl.ds(pl.multiple_of(t * TILE, TILE), TILE)
+            columns = columns_of(t)
             product = dot(
                 hidden[j, 0].reshape(2 * block, half), down[0:half, columns]
             ) + dot(hidden[j, 1].reshape(2 * block, half), down[half:units, columns])
@@ -348,58 +389,70 @@
             swap[k].wait_recv()
 
     local[0].wait()
+    tp[0, 0].wait_recv()
+    weights_here(0)
+    multiply_block(x, ny * (wide // TILE), wide // TILE)
+    send_part(0, 0, x, at_128(ny * wide, wide))
+    offer(2)
     arrive_across(0)
-    weights_here(0)
-    ready(0)
-    gate_and_up(0, 0)
+    arrive(1)
+    tp[0, 1].wait_recv()
+    multiply_block(nx, ny * (wide // TILE), wide // TILE)
+    send_part(1, 0, nx, at_128(ny * wide, wide))
     weights_here(1)
-    gate_and_up(0, 1)
-    arrive(1)
-    offer(2)
+    multiply(0, last // TILE, 2 * left // TILE)
+    send_part(2, 0, ny, slice(last, units))
+    weights_here(2)
+    multiply(0, y * (wide // TILE), wide // TILE)
     sum_weights()
-    activate(0, 0)
+    activate(0)
+    across(0)
+    activate(1)
     arrive_across(1)
-    ready(1)
-    gate_and_up(1, 0)
-    gate_and_up(1, 1)
+    gate_and_up(1)
+    activate(2)
     arrive(2)
     offer(3)
-    activate(0, 1)
-    hand_over(0, 0)
     total_weights()
+    hand_over(0)
+    activate(3)
     arrive_across(2)
-    ready(2)
-    gate_and_up(2, 0)
-    gate_and_up(2, 1)
+    gate_and_up(2)
+    activate(4)
     arrive(3)
-    activate(1, 0)
-    hand_over(0, 1)
-    activate(1, 1)
+    activate(5)
+    across(5)
+    activate(6)
+    across(6)
     arrive_across(3)
-    ready(3)
-    gate_and_up(3, 0)
-    gate_and_up(3, 1)
-    hand_over(1, 0)
+    gate_and_up(3)
+    across(3)
+    hand_over(5)
+    hand_over(6)
+    down_part(2)
+    activate(7)
+    across(7)
+    activate(8)
+    across(8)
+    across(4)
+    across(1)
+    across(2)
+    add_across(2)
+    checks(2)
+    hand_over(3)
+    hand_over(7)
+    hand_over(8)
+    down_part(3)
+    hand_over(4)
+    down_part(1)
+    add_across(3)
+    checks(3)
+    checks(1)
+    hand_over(1)
+    hand_over(2)
     down_part(0)
-    activate(2, 0)
-    hand_over(1, 1)
-    activate(2, 1)
-    down_part(1)
-    add_across(0)
+    add_across(1)
     checks(0)
-    hand_over(2, 0)
-    activate(3, 0)
-    hand_over(2, 1)
-    activate(3, 1)
-    add_across(1)
-    down_part(2)
-    checks(1)
-    checks(2)
-    add_across(2)
-    hand_over(3, 0)
-    hand_over(3, 1)
-    down_part(3)
-    checks(3)
 
     column_terms = dot(three_terms(unit_sums[0]), down[0:half, :]) + dot(
         three_terms(unit_sums[1]), down[half:units, :]
@@ -421,7 +474,7 @@
         )
         for k, slot in enumerate(small_slots)
     ]
-    add_across(3)
+    add_across(0)
     for copy in small:
         copy.wait_recv()
     total = small_recv[0]
@@ -440,6 +493,13 @@
         copy.wait_send()
 
 
+def write_results(mixed_ref, col_ref, row_ref, mixed_out, col_out, row_out):
+    mixed_out[...] = mixed_ref[...]
+    for k in range(col_ref.shape[0]):
+        col_out[pl.ds(k * 128, 128)] = col_ref[k]
+    row_out[...] = row_ref[0, 0 : row_out.shape[0]]
+
+
 def per_device_kernel(tokens, gate_up, down_weight):
     block, width = tokens.shape
     units = down_weight.shape[0]
@@ -449,7 +509,7 @@
     dma = pltpu.SemaphoreType.DMA
     bf16, f32 = jnp.bfloat16, jnp.float32
     sems = []
-    for count in (4, 3, 4, 8, 8, 8, 8, 8, 8, 6, 3, 7):
+    for count in (6, 3, 4, 8, 9, 9, 9, 9, 8, 6, 3, 7):
         sems += [dma((count,)), dma((count,))]
     mixed, col, row = pl.pallas_call(
         functools.partial(kernel, total_tokens, model_width),
@@ -466,7 +526,7 @@
             pltpu.VMEM((4, 2, 2, block, width), bf16),
             pltpu.VMEM((4, 2, block, units), f32),
             pltpu.VMEM((4, 2, block, units), bf16),
-            pltpu.VMEM((4, block, units), bf16),
+            pltpu.VMEM((4, 2, block, units), bf16),
             pltpu.VMEM((4, 2, 2, block, half), bf16),
             pltpu.VMEM((4, 2, block, width), f32),
             pltpu.VMEM((4, 2, block, width), bf16),
@@ -479,7 +539,7 @@
             pltpu.VMEM((2, 8, half), bf16),
             pltpu.VMEM((4, 2, 16, 128), f32),
             pltpu.VMEM((8, 16, 128), f32),
-            dma((6,)),
+            dma((8,)),
         ]
         + sems,
         compiler_params=pltpu.CompilerParams(
@@ -487,7 +547,15 @@
         ),
         name="swiglu_grid",
     )(tokens, gate_up, down_weight)
-    return mixed, col.reshape(width), row[0, :block]
+    return pl.pallas_call(
+        write_results,
+        out_shape=(
+            jax.ShapeDtypeStruct((block, width), bf16),
+            jax.ShapeDtypeStruct((width,), f32),
+            jax.ShapeDtypeStruct((block,), f32),
+        ),
+        name="write_results",
+    )(mixed, col, row)
 
 
 def fits_kernel(mesh):

time: 97.2 us -> 89.8 us (0.924)
  local copies, waits for them, and re-layouts: 4.1 us -> 0 us
  Pallas kernels: 92.2 us -> 89 us
    pallas_call x1, Pallas kernels: 92.2 us -> 87.4 us  [per_device_kernel(): pl.pallas_call(functools.partial(kernel, total_tokens, model_width), out_...]
    unnamed x2 -> x0, local copies, waits for them, and re-layouts: 2.91 us -> none
    pallas_call x0 -> x1, Pallas kernels: none -> 1.65 us  [per_device_kernel(): pl.pallas_call(write_results, out_shape=(jax.ShapeDtypeStruct((block, wid...]
    squeeze x1 -> x0, local copies, waits for them, and re-layouts: 1.19 us -> none  [per_device_kernel(): return (mixed, col.reshape(width), row[0, :block])]
where the time goes in v3:
time: 89.8 us; the launch traced here: 89.7 us
  Pallas kernels  89 us (99%)
    pallas_call x1, Pallas kernels, per_device_kernel(): pl.pallas_call(functools.partial(kernel, total_tokens, model_width), out_...  87.4 us

profile of v3, /device:TPU:0, one launch (start us, length us, event | category | flops | bytes accessed | tf_op | source)
XLA Modules:
  0.0 89.7 jit_solution(18193315084863005289)
XLA Ops:
  0.6 87.4 %swiglu_grid.1 = (bf16[112,1024]{1,0:T(8,128)(2,1)}, f32[8,128]{1,0:T(8,128)}, f32[8,128]{1,0:T(8,128)}) custom-call(bf16[112,1024]{1,0:T(8,128)(2,1)} %tokens_ref.1, bf16[2,1024,1792]{2,1,0:T(8,128)(2,1)} %gate_up_ref.1, bf16[1792,1024]{1,0:T(8,128)(2,1)} %down_ref.1), custom_call_target="tpu_custom_call" | custom-call | tf_op jit(solution)/shard_map/swiglu_grid/pallas_call | solution.py:514
  88.0 1.7 %write_results.1 = (bf16[112,1024]{1,0:T(8,128)(2,1)}, f32[1024]{0:T(1024)}, f32[112]{0:T(128)}) custom-call(bf16[112,1024]{1,0:T(8,128)(2,1)} %get-tuple-element.6.mixed_ref, f32[8,128]{1,0:T(8,128)} %get-tuple-element.7.col_ref, f32[8,128]{1,0:T(8,128)} %get-tuple-element.8.row_ref), custom_call_target="tpu_custom_call" | custom-call | tf_op jit(solution)/shard_map/write_results/pallas_call | solution.py:550

commit v4 on v3

--- a/solution.py
+++ b/solution.py
@@ -140,7 +140,7 @@
     group = half // 256 * 128
     left = half - 2 * group
     wide, last = 2 * group, 4 * group
-    strip = width // 2
+    strips = (2, 4, 2, 2)
     x = lax.axis_index("dp")
     row = lax.axis_index("row")
     z = lax.axis_index("col")
@@ -203,6 +203,7 @@
     ]
 
     unit_sums[...] = jnp.zeros_like(unit_sums)
+    weight_parts[row] = jnp.zeros((16, 128), jnp.float32)
     small_send[...] = jnp.zeros_like(small_send)
 
     weight_copies = []
@@ -211,7 +212,10 @@
         local[7].wait()
         ones_width = jnp.ones((8, width), jnp.bfloat16)
         for h in range(2):
-            weight_parts[row, h] = dot_rows(ones_width, down[h * half : (h + 1) * half, :])
+            sums = dot_rows(ones_width, down[h * half : (h + 1) * half, :])
+            for k in range(half // 128):
+                line = slice(8 * h + k, 8 * h + k + 1)
+                weight_parts[row, line, :] = sums[0:1, k * 128 : (k + 1) * 128]
         place = weight_parts.at[row]
         for k in range(3):
             weight_copies.append(send(place, place, ws_send.at[k], ws_recv.at[k], rows[k]))
@@ -219,10 +223,12 @@
     def total_weights():
         for copy in weight_copies:
             copy.wait_recv()
+        total = weight_parts[0] + weight_parts[1] + weight_parts[2] + weight_parts[3]
         for h in range(2):
-            weight_terms[h] = three_terms(
-                weight_parts[0, h] + weight_parts[1, h] + weight_parts[2, h] + weight_parts[3, h]
+            sums = jnp.concatenate(
+                [total[8 * h + k : 8 * h + k + 1, :] for k in range(half // 128)], axis=1
             )
+            weight_terms[h] = three_terms(jnp.broadcast_to(sums, (8, half)))
 
     def arrive(j):
         tz[j].wait_recv()
@@ -328,8 +334,23 @@
         multiply(j, wide // TILE, (units - wide) // TILE)
         send_part(2 + 2 * j, j, ny, slice(wide, units))
 
+    def strips_of(j):
+        step = width // strips[j]
+        return [
+            (sum(strips[:j]) + q, slice(q * step, (q + 1) * step)) for q in range(strips[j])
+        ]
+
+    def send_across(j, n, place):
+        mx[n] = send(
+            out_send.at[j, nx, :, place],
+            x_recv.at[j, :, place],
+            mx_send.at[n],
+            mx_recv.at[n],
+            across_x,
+        )
+
     def down_part(j):
-        for n in (0, 1, 2) if j == 0 else (1 + 2 * j, 2 + 2 * j):
+        for n in (1 + 2 * j, 2 + 2 * j):
             hp[n].wait_recv()
             hf[n].wait_recv()
 
@@ -343,17 +364,34 @@
             out_send[j, :, :, columns] = product.astype(jnp.bfloat16)
             return carry
 
-        for q in range(2):
-            lax.fori_loop(q * strip // TILE, (q + 1) * strip // TILE, body, 0)
-            place = slice(q * strip, (q + 1) * strip)
-            n = 2 * j + q
-            mx[j, q] = send(
-                out_send.at[j, nx, :, place],
-                x_recv.at[j, :, place],
-                mx_send.at[n],
-                mx_recv.at[n],
-                across_x,
+        for n, place in strips_of(j):
+            lax.fori_loop(place.start // TILE, place.stop // TILE, body, 0)
+            send_across(j, n, place)
+
+    def down_block(b, place):
+        def body(t, carry):
+            columns = columns_of(t)
+            product = dot(hidden[0, 0, b], down[0:half, columns]) + dot(
+                hidden[0, 1, b], down[half:units, columns]
             )
+            out_wide[0, b, :, columns] = product
+            out_send[0, b, :, columns] = product.astype(jnp.bfloat16)
+            return carry
+
+        lax.fori_loop(place.start // TILE, place.stop // TILE, body, 0)
+
+    def down_across():
+        for n in (1, 2):
+            hp[n].wait_recv()
+            hf[n].wait_recv()
+        for n, place in strips_of(0):
+            down_block(nx, place)
+            send_across(0, n, place)
+
+    def down_own():
+        hp[0].wait_recv()
+        hf[0].wait_recv()
+        down_block(x, slice(0, width))
 
     def checks(j):
         ones = jnp.ones((8, 2 * block), jnp.bfloat16)
@@ -366,20 +404,18 @@
             small_send[j, b, 8:9, 0:block] = jnp.sum(terms, axis=0, keepdims=True)
 
     def add_across(j):
-        for q in range(2):
-            mx[j, q].wait_recv()
-            place = slice(q * strip, (q + 1) * strip)
+        for n, place in strips_of(j):
+            mx[n].wait_recv()
             value = out_wide[j, x, :, place] + x_recv[j, :, place].astype(jnp.float32)
             if j == 0:
                 own_sum[:, place] = value
             else:
                 z_send[j - 1, :, place] = value.astype(jnp.bfloat16)
-                n = 2 * (j - 1) + q
-                mz[j, q] = send(
+                mz[n] = send(
                     z_send.at[j - 1, :, place],
                     z_recv.at[j - 1, :, place],
-                    mz_send.at[n],
-                    mz_recv.at[n],
+                    mz_send.at[n - strips[0]],
+                    mz_recv.at[n - strips[0]],
                     peers[j - 1],
                 )
 
@@ -406,15 +442,15 @@
     multiply(0, y * (wide // TILE), wide // TILE)
     sum_weights()
     activate(0)
-    across(0)
     activate(1)
+    across(1)
     arrive_across(1)
     gate_and_up(1)
     activate(2)
     arrive(2)
     offer(3)
     total_weights()
-    hand_over(0)
+    hand_over(1)
     activate(3)
     arrive_across(2)
     gate_and_up(2)
@@ -422,10 +458,10 @@
     arrive(3)
     activate(5)
     across(5)
+    arrive_across(3)
+    gate_and_up(3)
     activate(6)
     across(6)
-    arrive_across(3)
-    gate_and_up(3)
     across(3)
     hand_over(5)
     hand_over(6)
@@ -435,8 +471,8 @@
     activate(8)
     across(8)
     across(4)
-    across(1)
     across(2)
+    across(0)
     add_across(2)
     checks(2)
     hand_over(3)
@@ -446,12 +482,13 @@
     hand_over(4)
     down_part(1)
     add_across(3)
+    hand_over(2)
+    down_across()
     checks(3)
+    add_across(1)
     checks(1)
-    hand_over(1)
-    hand_over(2)
-    down_part(0)
-    add_across(1)
+    hand_over(0)
+    down_own()
     checks(0)
 
     column_terms = dot(three_terms(unit_sums[0]), down[0:half, :]) + dot(
@@ -482,13 +519,15 @@
         total = total + small_recv[k]
     col_ref[...] = total[0:8] / math.sqrt(total_tokens)
     row_ref[...] = total[8:16] / math.sqrt(model_width)
-    for q in range(2):
-        place = slice(q * strip, (q + 1) * strip)
-        value = own_sum[:, place]
-        for j in range(1, 4):
-            mz[j, q].wait_recv()
-            value = value + z_recv[j - 1, :, place].astype(jnp.float32)
-        mixed_ref[:, place] = value.astype(jnp.bfloat16)
+    for j in range(1, 4):
+        for n, _ in strips_of(j):
+            mz[n].wait_recv()
+    mixed_ref[...] = (
+        own_sum[...]
+        + z_recv[0].astype(jnp.float32)
+        + z_recv[1].astype(jnp.float32)
+        + z_recv[2].astype(jnp.float32)
+    ).astype(jnp.bfloat16)
     for copy in sent:
         copy.wait_send()
 
@@ -509,7 +548,7 @@
     dma = pltpu.SemaphoreType.DMA
     bf16, f32 = jnp.bfloat16, jnp.float32
     sems = []
-    for count in (6, 3, 4, 8, 9, 9, 9, 9, 8, 6, 3, 7):
+    for count in (6, 3, 4, 8, 9, 9, 9, 9, 10, 8, 3, 7):
         sems += [dma((count,)), dma((count,))]
     mixed, col, row = pl.pallas_call(
         functools.partial(kernel, total_tokens, model_width),
@@ -535,7 +574,7 @@
             pltpu.VMEM((3, block, width), bf16),
             pltpu.VMEM((block, width), f32),
             pltpu.VMEM((2, 8, half), f32),
-            pltpu.VMEM((4, 2, 8, half), f32),
+            pltpu.VMEM((4, 16, 128), f32),
             pltpu.VMEM((2, 8, half), bf16),
             pltpu.VMEM((4, 2, 16, 128), f32),
             pltpu.VMEM((8, 16, 128), f32),

time: 89.8 us -> 94.3 us (1.050)
  Pallas kernels: 89 us -> 93.5 us
    pallas_call x1, Pallas kernels: 87.4 us -> 91.9 us  [per_device_kernel(): pl.pallas_call(functools.partial(kernel, total_tokens, model_width), out_...]
where the time goes in v4:
time: 94.3 us; the launch traced here: 94.2 us
  Pallas kernels  93.5 us (99%)
    pallas_call x1, Pallas kernels, per_device_kernel(): pl.pallas_call(functools.partial(kernel, total_tokens, model_width), out_...  91.9 us

profile of v4, /device:TPU:0, one launch (start us, length us, event | category | flops | bytes accessed | tf_op | source)
XLA Modules:
  0.0 94.2 jit_solution(15519639029132638406)
XLA Ops:
  0.6 91.9 %swiglu_grid.1 = (bf16[112,1024]{1,0:T(8,128)(2,1)}, f32[8,128]{1,0:T(8,128)}, f32[8,128]{1,0:T(8,128)}) custom-call(bf16[112,1024]{1,0:T(8,128)(2,1)} %tokens_ref.1, bf16[2,1024,1792]{2,1,0:T(8,128)(2,1)} %gate_up_ref.1, bf16[1792,1024]{1,0:T(8,128)(2,1)} %down_ref.1), custom_call_target="tpu_custom_call" | custom-call | tf_op jit(solution)/shard_map/swiglu_grid/pallas_call | solution.py:553
  92.5 1.7 %write_results.1 = (bf16[112,1024]{1,0:T(8,128)(2,1)}, f32[1024]{0:T(1024)}, f32[112]{0:T(128)}) custom-call(bf16[112,1024]{1,0:T(8,128)(2,1)} %get-tuple-element.6.mixed_ref, f32[8,128]{1,0:T(8,128)} %get-tuple-element.7.col_ref, f32[8,128]{1,0:T(8,128)} %get-tuple-element.8.row_ref), custom_call_target="tpu_custom_call" | custom-call | tf_op jit(solution)/shard_map/write_results/pallas_call | solution.py:589

commit v5 on v4

--- a/solution.py
+++ b/solution.py
@@ -196,7 +196,7 @@
             tokens_ref, acts.at[z, core, x], tz_send.at[j - 1], tz_recv.at[j - 1], peers[j - 1]
         )
 
-    offer(1)
+    offer(2)
     swap = [
         send(src, dst, w_send.at[k], w_recv.at[k], partner)
         for k, (src, dst) in enumerate(weight_slices(ncore))
@@ -332,6 +332,8 @@
         multiply(j, 0, wide // TILE)
         send_part(1 + 2 * j, j, ny, slice(0, wide))
         multiply(j, wide // TILE, (units - wide) // TILE)
+
+    def send_rest(j):
         send_part(2 + 2 * j, j, ny, slice(wide, units))
 
     def strips_of(j):
@@ -429,67 +431,70 @@
     weights_here(0)
     multiply_block(x, ny * (wide // TILE), wide // TILE)
     send_part(0, 0, x, at_128(ny * wide, wide))
-    offer(2)
     arrive_across(0)
-    arrive(1)
     tp[0, 1].wait_recv()
     multiply_block(nx, ny * (wide // TILE), wide // TILE)
     send_part(1, 0, nx, at_128(ny * wide, wide))
     weights_here(1)
     multiply(0, last // TILE, 2 * left // TILE)
     send_part(2, 0, ny, slice(last, units))
+    offer(3)
     weights_here(2)
     multiply(0, y * (wide // TILE), wide // TILE)
     sum_weights()
     activate(0)
+    across(0)
+    arrive(2)
+    offer(1)
     activate(1)
     across(1)
-    arrive_across(1)
-    gate_and_up(1)
     activate(2)
-    arrive(2)
-    offer(3)
-    total_weights()
-    hand_over(1)
-    activate(3)
+    across(2)
     arrive_across(2)
     gate_and_up(2)
-    activate(4)
+    send_rest(2)
+    total_weights()
+    hand_over(0)
+    hand_over(1)
+    hand_over(2)
     arrive(3)
     activate(5)
     across(5)
     arrive_across(3)
     gate_and_up(3)
+    send_rest(3)
+    arrive(1)
     activate(6)
     across(6)
-    across(3)
-    hand_over(5)
-    hand_over(6)
-    down_part(2)
+    down_across()
+    down_own()
+    arrive_across(1)
+    gate_and_up(1)
     activate(7)
     across(7)
     activate(8)
     across(8)
-    across(4)
-    across(2)
-    across(0)
-    add_across(2)
-    checks(2)
-    hand_over(3)
+    send_rest(1)
+    hand_over(5)
+    hand_over(6)
+    down_part(2)
+    activate(3)
+    across(3)
+    checks(0)
+    add_across(0)
     hand_over(7)
     hand_over(8)
     down_part(3)
+    add_across(2)
+    activate(4)
+    across(4)
+    checks(2)
+    checks(3)
+    add_across(3)
+    hand_over(3)
     hand_over(4)
     down_part(1)
-    add_across(3)
-    hand_over(2)
-    down_across()
-    checks(3)
-    add_across(1)
     checks(1)
-    hand_over(0)
-    down_own()
-    checks(0)
 
     column_terms = dot(three_terms(unit_sums[0]), down[0:half, :]) + dot(
         three_terms(unit_sums[1]), down[half:units, :]
@@ -511,7 +516,7 @@
         )
         for k, slot in enumerate(small_slots)
     ]
-    add_across(0)
+    add_across(1)
     for copy in small:
         copy.wait_recv()
     total = small_recv[0]

time: 94.3 us -> 88.6 us (0.940)
  Pallas kernels: 93.5 us -> 87.8 us
    pallas_call x1, Pallas kernels: 91.9 us -> 86.1 us  [per_device_kernel(): pl.pallas_call(functools.partial(kernel, total_tokens, model_width), out_...]
where the time goes in v5:
time: 88.6 us; the launch traced here: 88.4 us
  Pallas kernels  87.8 us (99%)
    pallas_call x1, Pallas kernels, per_device_kernel(): pl.pallas_call(functools.partial(kernel, total_tokens, model_width), out_...  86.1 us

profile of v5, /device:TPU:0, one launch (start us, length us, event | category | flops | bytes accessed | tf_op | source)
XLA Modules:
  0.0 88.4 jit_solution(14959695059562309419)
XLA Ops:
  0.6 86.1 %swiglu_grid.1 = (bf16[112,1024]{1,0:T(8,128)(2,1)}, f32[8,128]{1,0:T(8,128)}, f32[8,128]{1,0:T(8,128)}) custom-call(bf16[112,1024]{1,0:T(8,128)(2,1)} %tokens_ref.1, bf16[2,1024,1792]{2,1,0:T(8,128)(2,1)} %gate_up_ref.1, bf16[1792,1024]{1,0:T(8,128)(2,1)} %down_ref.1), custom_call_target="tpu_custom_call" | custom-call | tf_op jit(solution)/shard_map/swiglu_grid/pallas_call | solution.py:558
  86.8 1.7 %write_results.1 = (bf16[112,1024]{1,0:T(8,128)(2,1)}, f32[1024]{0:T(1024)}, f32[112]{0:T(128)}) custom-call(bf16[112,1024]{1,0:T(8,128)(2,1)} %get-tuple-element.6.mixed_ref, f32[8,128]{1,0:T(8,128)} %get-tuple-element.7.col_ref, f32[8,128]{1,0:T(8,128)} %get-tuple-element.8.row_ref), custom_call_target="tpu_custom_call" | custom-call | tf_op jit(solution)/shard_map/write_results/pallas_call | solution.py:594

commit v6 on v5

--- a/solution.py
+++ b/solution.py
@@ -108,6 +108,8 @@
     weight_terms,
     small_send,
     small_recv,
+    unit_terms,
+    column_sums,
     local_sem,
     w_send,
     w_recv,
@@ -250,6 +252,9 @@
     def columns_of(tile):
         return pl.ds(pl.multiple_of(tile * TILE, TILE), TILE)
 
+    def both(ref, one, other):
+        return jnp.concatenate([ref[one], ref[other]], axis=0)
+
     def multiply_block(b, tile, tiles):
         def body(t, carry):
             columns = columns_of(tile + t)
@@ -259,20 +264,22 @@
             part_send[0, b, :, columns] = product.astype(jnp.bfloat16)
             return carry
 
-        lax.fori_loop(0, tiles, body, 0)
-
-    def multiply(j, tile, tiles):
+        lax.fori_loop(0, tiles, body, 0, unroll=True)
+
+    def multiply(j, tile, tiles, keep_both=False):
         def body(t, carry):
             columns = columns_of(tile + t)
-            product = dot(
-                acts[zs[j], 0].reshape(2 * block, width), weights[0, :, columns]
-            ) + dot(acts[zs[j], 1].reshape(2 * block, width), weights[1, :, columns])
-            product = product.reshape(2, block, TILE)
-            part_wide[j, :, :, columns] = product
-            part_send[j, :, :, columns] = product.astype(jnp.bfloat16)
+            product = dot(both(acts.at[zs[j], 0], ny, y), weights[0, :, columns]) + dot(
+                both(acts.at[zs[j], 1], ny, y), weights[1, :, columns]
+            )
+            if keep_both:
+                part_wide[j, ny, :, columns] = product[:block]
+            else:
+                part_send[j, ny, :, columns] = product[:block].astype(jnp.bfloat16)
+            part_wide[j, y, :, columns] = product[block:]
             return carry
 
-        lax.fori_loop(0, tiles, body, 0)
+        lax.fori_loop(0, tiles, body, 0, unroll=True)
 
     def send_part(n, j, b, place):
         py[n] = send(
@@ -351,23 +358,34 @@
             across_x,
         )
 
-    def down_part(j):
+    def down_part(j, column_terms=False):
         for n in (1 + 2 * j, 2 + 2 * j):
             hp[n].wait_recv()
             hf[n].wait_recv()
+        if column_terms:
+            add_units(j)
+            for h in range(2):
+                unit_terms[h] = three_terms(unit_sums[h])
+
+        def rows_of(h):
+            chunk = both(hidden.at[j, h], nx, x)
+            return jnp.concatenate([chunk, unit_terms[h]], axis=0) if column_terms else chunk
 
         def body(t, carry):
             columns = columns_of(t)
-            product = dot(
-                hidden[j, 0].reshape(2 * block, half), down[0:half, columns]
-            ) + dot(hidden[j, 1].reshape(2 * block, half), down[half:units, columns])
-            product = product.reshape(2, block, TILE)
-            out_wide[j, :, :, columns] = product
-            out_send[j, :, :, columns] = product.astype(jnp.bfloat16)
+            product = dot(rows_of(0), down[0:half, columns]) + dot(
+                rows_of(1), down[half:units, columns]
+            )
+            out_send[j, nx, :, columns] = product[:block].astype(jnp.bfloat16)
+            out_wide[j, x, :, columns] = product[block : 2 * block]
+            if column_terms:
+                column_sums[:, columns] = jnp.sum(
+                    product[2 * block :].reshape(2, 8, TILE), axis=0
+                )
             return carry
 
         for n, place in strips_of(j):
-            lax.fori_loop(place.start // TILE, place.stop // TILE, body, 0)
+            lax.fori_loop(place.start // TILE, place.stop // TILE, body, 0, unroll=True)
             send_across(j, n, place)
 
     def down_block(b, place):
@@ -380,7 +398,7 @@
             out_send[0, b, :, columns] = product.astype(jnp.bfloat16)
             return carry
 
-        lax.fori_loop(place.start // TILE, place.stop // TILE, body, 0)
+        lax.fori_loop(place.start // TILE, place.stop // TILE, body, 0, unroll=True)
 
     def down_across():
         for n in (1, 2):
@@ -395,15 +413,21 @@
         hf[0].wait_recv()
         down_block(x, slice(0, width))
 
-    def checks(j):
-        ones = jnp.ones((8, 2 * block), jnp.bfloat16)
+    def add_units(j):
+        ones = jnp.ones((16, 2 * block), jnp.bfloat16)
         for h in range(2):
             unit_sums[h] += dot(ones, hidden[j, h].reshape(2 * block, half))
+
+    def add_tokens(j):
         for b in range(2):
             terms = dot_rows(weight_terms[0], hidden[j, 0, b]) + dot_rows(
                 weight_terms[1], hidden[j, 1, b]
             )
             small_send[j, b, 8:9, 0:block] = jnp.sum(terms, axis=0, keepdims=True)
+
+    def checks(j):
+        add_units(j)
+        add_tokens(j)
 
     def add_across(j):
         for n, place in strips_of(j):
@@ -440,7 +464,7 @@
     send_part(2, 0, ny, slice(last, units))
     offer(3)
     weights_here(2)
-    multiply(0, y * (wide // TILE), wide // TILE)
+    multiply(0, y * (wide // TILE), wide // TILE, keep_both=True)
     sum_weights()
     activate(0)
     across(0)
@@ -493,13 +517,10 @@
     add_across(3)
     hand_over(3)
     hand_over(4)
-    down_part(1)
-    checks(1)
-
-    column_terms = dot(three_terms(unit_sums[0]), down[0:half, :]) + dot(
-        three_terms(unit_sums[1]), down[half:units, :]
-    )
-    columns = jnp.sum(column_terms, axis=0, keepdims=True)
+    down_part(1, column_terms=True)
+    add_tokens(1)
+
+    columns = jnp.sum(column_sums[...], axis=0, keepdims=True)
     for j in range(4):
         for b in range(2):
             for k in range(width // 128):
@@ -578,11 +599,13 @@
             pltpu.VMEM((3, block, width), bf16),
             pltpu.VMEM((3, block, width), bf16),
             pltpu.VMEM((block, width), f32),
-            pltpu.VMEM((2, 8, half), f32),
+            pltpu.VMEM((2, 16, half), f32),
             pltpu.VMEM((4, 16, 128), f32),
             pltpu.VMEM((2, 8, half), bf16),
             pltpu.VMEM((4, 2, 16, 128), f32),
             pltpu.VMEM((8, 16, 128), f32),
+            pltpu.VMEM((2, 16, half), bf16),
+            pltpu.VMEM((8, width), f32),
             dma((8,)),
         ]
         + sems,

time: 88.6 us -> 88.2 us (level)
  no operation moved by 1% of the time
where the time goes in v6:
time: 88.2 us; the launch traced here: 88.1 us
  Pallas kernels  87.4 us (99%)
    pallas_call x1, Pallas kernels, per_device_kernel(): pl.pallas_call(functools.partial(kernel, total_tokens, model_width), out_...  85.8 us

profile of v6, /device:TPU:0, one launch (start us, length us, event | category | flops | bytes accessed | tf_op | source)
XLA Modules:
  0.0 88.1 jit_solution(6882618485529478372)
XLA Ops:
  0.6 85.8 %swiglu_grid.1 = (bf16[112,1024]{1,0:T(8,128)(2,1)}, f32[8,128]{1,0:T(8,128)}, f32[8,128]{1,0:T(8,128)}) custom-call(bf16[112,1024]{1,0:T(8,128)(2,1)} %tokens_ref.1, bf16[2,1024,1792]{2,1,0:T(8,128)(2,1)} %gate_up_ref.1, bf16[1792,1024]{1,0:T(8,128)(2,1)} %down_ref.1), custom_call_target="tpu_custom_call" | custom-call | tf_op jit(solution)/shard_map/swiglu_grid/pallas_call | solution.py:579
  86.4 1.7 %write_results.1 = (bf16[112,1024]{1,0:T(8,128)(2,1)}, f32[1024]{0:T(1024)}, f32[112]{0:T(128)}) custom-call(bf16[112,1024]{1,0:T(8,128)(2,1)} %get-tuple-element.6.mixed_ref, f32[8,128]{1,0:T(8,128)} %get-tuple-element.7.col_ref, f32[8,128]{1,0:T(8,128)} %get-tuple-element.8.row_ref), custom_call_target="tpu_custom_call" | custom-call | tf_op jit(solution)/shard_map/write_results/pallas_call | solution.py:617

commit v7 on v6

--- a/solution.py
+++ b/solution.py
@@ -198,7 +198,7 @@
             tokens_ref, acts.at[z, core, x], tz_send.at[j - 1], tz_recv.at[j - 1], peers[j - 1]
         )
 
-    offer(2)
+    offer(1)
     swap = [
         send(src, dst, w_send.at[k], w_recv.at[k], partner)
         for k, (src, dst) in enumerate(weight_slices(ncore))
@@ -334,10 +334,11 @@
         place = hidden_place(n, ny)
         hf[n] = send(place, place, hf_send.at[n], hf_recv.at[n], partner)
 
-    def gate_and_up(j):
-        ready(j)
+    def first_part(j):
         multiply(j, 0, wide // TILE)
         send_part(1 + 2 * j, j, ny, slice(0, wide))
+
+    def rest_part(j):
         multiply(j, wide // TILE, (units - wide) // TILE)
 
     def send_rest(j):
@@ -358,60 +359,61 @@
             across_x,
         )
 
-    def down_part(j, column_terms=False):
+    def down_part(j):
         for n in (1 + 2 * j, 2 + 2 * j):
             hp[n].wait_recv()
             hf[n].wait_recv()
-        if column_terms:
-            add_units(j)
-            for h in range(2):
-                unit_terms[h] = three_terms(unit_sums[h])
+
+        def body(t, carry):
+            columns = columns_of(t)
+            product = dot(both(hidden.at[j, 0], nx, x), down[0:half, columns]) + dot(
+                both(hidden.at[j, 1], nx, x), down[half:units, columns]
+            )
+            out_send[j, nx, :, columns] = product[:block].astype(jnp.bfloat16)
+            out_wide[j, x, :, columns] = product[block:]
+            return carry
+
+        for n, place in strips_of(j):
+            lax.fori_loop(place.start // TILE, place.stop // TILE, body, 0, unroll=True)
+            send_across(j, n, place)
+
+    def down_across():
+        for n in (1, 2):
+            hp[n].wait_recv()
+            hf[n].wait_recv()
+
+        def body(t, carry):
+            columns = columns_of(t)
+            product = dot(hidden[0, 0, nx], down[0:half, columns]) + dot(
+                hidden[0, 1, nx], down[half:units, columns]
+            )
+            out_send[0, nx, :, columns] = product.astype(jnp.bfloat16)
+            return carry
+
+        for n, place in strips_of(0):
+            lax.fori_loop(place.start // TILE, place.stop // TILE, body, 0, unroll=True)
+            send_across(0, n, place)
+
+    def down_own():
+        hp[0].wait_recv()
+        hf[0].wait_recv()
+        add_units(0)
+        for h in range(2):
+            unit_terms[h] = three_terms(unit_sums[h])
 
         def rows_of(h):
-            chunk = both(hidden.at[j, h], nx, x)
-            return jnp.concatenate([chunk, unit_terms[h]], axis=0) if column_terms else chunk
+            return jnp.concatenate([hidden[0, h, x], unit_terms[h]], axis=0)
 
         def body(t, carry):
             columns = columns_of(t)
             product = dot(rows_of(0), down[0:half, columns]) + dot(
                 rows_of(1), down[half:units, columns]
             )
-            out_send[j, nx, :, columns] = product[:block].astype(jnp.bfloat16)
-            out_wide[j, x, :, columns] = product[block : 2 * block]
-            if column_terms:
-                column_sums[:, columns] = jnp.sum(
-                    product[2 * block :].reshape(2, 8, TILE), axis=0
-                )
+            out_wide[0, x, :, columns] = product[:block]
+            column_sums[:, columns] = jnp.sum(product[block:].reshape(2, 8, TILE), axis=0)
             return carry
 
-        for n, place in strips_of(j):
-            lax.fori_loop(place.start // TILE, place.stop // TILE, body, 0, unroll=True)
-            send_across(j, n, place)
-
-    def down_block(b, place):
-        def body(t, carry):
-            columns = columns_of(t)
-            product = dot(hidden[0, 0, b], down[0:half, columns]) + dot(
-                hidden[0, 1, b], down[half:units, columns]
-            )
-            out_wide[0, b, :, columns] = product
-            out_send[0, b, :, columns] = product.astype(jnp.bfloat16)
-            return carry
-
-        lax.fori_loop(place.start // TILE, place.stop // TILE, body, 0, unroll=True)
-
-    def down_across():
-        for n in (1, 2):
-            hp[n].wait_recv()
-            hf[n].wait_recv()
-        for n, place in strips_of(0):
-            down_block(nx, place)
-            send_across(0, n, place)
-
-    def down_own():
-        hp[0].wait_recv()
-        hf[0].wait_recv()
-        down_block(x, slice(0, width))
+        lax.fori_loop(0, width // TILE, body, 0, unroll=True)
 
     def add_units(j):
         ones = jnp.ones((16, 2 * block), jnp.bfloat16)
@@ -455,70 +457,75 @@
     weights_here(0)
     multiply_block(x, ny * (wide // TILE), wide // TILE)
     send_part(0, 0, x, at_128(ny * wide, wide))
+    offer(2)
     arrive_across(0)
+    arrive(1)
     tp[0, 1].wait_recv()
     multiply_block(nx, ny * (wide // TILE), wide // TILE)
     send_part(1, 0, nx, at_128(ny * wide, wide))
     weights_here(1)
     multiply(0, last // TILE, 2 * left // TILE)
     send_part(2, 0, ny, slice(last, units))
-    offer(3)
     weights_here(2)
     multiply(0, y * (wide // TILE), wide // TILE, keep_both=True)
     sum_weights()
     activate(0)
-    across(0)
-    arrive(2)
-    offer(1)
+    offer(3)
+    arrive_across(1)
+    ready(1)
+    first_part(1)
     activate(1)
     across(1)
+    arrive(2)
     activate(2)
-    across(2)
+    rest_part(1)
+    total_weights()
     arrive_across(2)
-    gate_and_up(2)
+    ready(2)
+    first_part(2)
+    rest_part(2)
     send_rest(2)
-    total_weights()
-    hand_over(0)
     hand_over(1)
-    hand_over(2)
     arrive(3)
+    activate(3)
     activate(5)
     across(5)
     arrive_across(3)
-    gate_and_up(3)
+    ready(3)
+    first_part(3)
+    rest_part(3)
     send_rest(3)
-    arrive(1)
     activate(6)
     across(6)
-    down_across()
-    down_own()
-    arrive_across(1)
-    gate_and_up(1)
     activate(7)
     across(7)
+    hand_over(5)
     activate(8)
     across(8)
     send_rest(1)
-    hand_over(5)
+    across(3)
     hand_over(6)
     down_part(2)
-    activate(3)
-    across(3)
-    checks(0)
-    add_across(0)
+    checks(2)
     hand_over(7)
     hand_over(8)
     down_part(3)
     add_across(2)
     activate(4)
     across(4)
-    checks(2)
+    across(2)
+    across(0)
     checks(3)
     add_across(3)
     hand_over(3)
     hand_over(4)
-    down_part(1, column_terms=True)
-    add_tokens(1)
+    down_part(1)
+    hand_over(2)
+    down_across()
+    checks(1)
+    hand_over(0)
+    down_own()
+    add_tokens(0)
 
     columns = jnp.sum(column_sums[...], axis=0, keepdims=True)
     for j in range(4):
@@ -538,6 +545,7 @@
         for k, slot in enumerate(small_slots)
     ]
     add_across(1)
+    add_across(0)
     for copy in small:
         copy.wait_recv()
     total = small_recv[0]

time: 88.2 us -> 93.5 us (1.060)
  Pallas kernels: 87.4 us -> 92.7 us
    pallas_call x1, Pallas kernels: 85.8 us -> 91 us  [per_device_kernel(): pl.pallas_call(functools.partial(kernel, total_tokens, model_width), out_...]
where the time goes in v7:
time: 93.5 us; the launch traced here: 93.3 us
  Pallas kernels  92.7 us (99%)
    pallas_call x1, Pallas kernels, per_device_kernel(): pl.pallas_call(functools.partial(kernel, total_tokens, model_width), out_...  91 us

profile of v7, /device:TPU:0, one launch (start us, length us, event | category | flops | bytes accessed | tf_op | source)
XLA Modules:
  0.0 93.3 jit_solution(5744315130631598666)
XLA Ops:
  0.6 91.0 %swiglu_grid.1 = (bf16[112,1024]{1,0:T(8,128)(2,1)}, f32[8,128]{1,0:T(8,128)}, f32[8,128]{1,0:T(8,128)}) custom-call(bf16[112,1024]{1,0:T(8,128)(2,1)} %tokens_ref.1, bf16[2,1024,1792]{2,1,0:T(8,128)(2,1)} %gate_up_ref.1, bf16[1792,1024]{1,0:T(8,128)(2,1)} %down_ref.1), custom_call_target="tpu_custom_call" | custom-call | tf_op jit(solution)/shard_map/swiglu_grid/pallas_call | solution.py:587
  91.6 1.7 %write_results.1 = (bf16[112,1024]{1,0:T(8,128)(2,1)}, f32[1024]{0:T(1024)}, f32[112]{0:T(128)}) custom-call(bf16[112,1024]{1,0:T(8,128)(2,1)} %get-tuple-element.6.mixed_ref, f32[8,128]{1,0:T(8,128)} %get-tuple-element.7.col_ref, f32[8,128]{1,0:T(8,128)} %get-tuple-element.8.row_ref), custom_call_target="tpu_custom_call" | custom-call | tf_op jit(solution)/shard_map/write_results/pallas_call | solution.py:625

commit v8 on v6

--- a/solution.py
+++ b/solution.py
@@ -142,7 +142,7 @@
     group = half // 256 * 128
     left = half - 2 * group
     wide, last = 2 * group, 4 * group
-    strips = (2, 4, 2, 2)
+    strips = (2, 4, 2, 4)
     x = lax.axis_index("dp")
     row = lax.axis_index("row")
     z = lax.axis_index("col")
@@ -455,6 +455,7 @@
     weights_here(0)
     multiply_block(x, ny * (wide // TILE), wide // TILE)
     send_part(0, 0, x, at_128(ny * wide, wide))
+    offer(3)
     arrive_across(0)
     tp[0, 1].wait_recv()
     multiply_block(nx, ny * (wide // TILE), wide // TILE)
@@ -462,14 +463,13 @@
     weights_here(1)
     multiply(0, last // TILE, 2 * left // TILE)
     send_part(2, 0, ny, slice(last, units))
-    offer(3)
     weights_here(2)
     multiply(0, y * (wide // TILE), wide // TILE, keep_both=True)
+    offer(1)
     sum_weights()
     activate(0)
     across(0)
     arrive(2)
-    offer(1)
     activate(1)
     across(1)
     activate(2)
@@ -496,9 +496,9 @@
     gate_and_up(1)
     activate(7)
     across(7)
+    send_rest(1)
     activate(8)
     across(8)
-    send_rest(1)
     hand_over(5)
     hand_over(6)
     down_part(2)
@@ -574,7 +574,7 @@
     dma = pltpu.SemaphoreType.DMA
     bf16, f32 = jnp.bfloat16, jnp.float32
     sems = []
-    for count in (6, 3, 4, 8, 9, 9, 9, 9, 10, 8, 3, 7):
+    for count in (6, 3, 4, 8, 9, 9, 9, 9, 12, 10, 3, 7):
         sems += [dma((count,)), dma((count,))]
     mixed, col, row = pl.pallas_call(
         functools.partial(kernel, total_tokens, model_width),

time: 88.2 us -> 93.8 us (1.063)
  Pallas kernels: 87.4 us -> 93 us
    pallas_call x1, Pallas kernels: 85.8 us -> 91.3 us  [per_device_kernel(): pl.pallas_call(functools.partial(kernel, total_tokens, model_width), out_...]
where the time goes in v8:
time: 93.8 us; the launch traced here: 93.6 us
  Pallas kernels  93 us (99%)
    pallas_call x1, Pallas kernels, per_device_kernel(): pl.pallas_call(functools.partial(kernel, total_tokens, model_width), out_...  91.3 us

profile of v8, /device:TPU:0, one launch (start us, length us, event | category | flops | bytes accessed | tf_op | source)
XLA Modules:
  0.0 93.6 jit_solution(15326951643000626342)
XLA Ops:
  0.6 91.3 %swiglu_grid.1 = (bf16[112,1024]{1,0:T(8,128)(2,1)}, f32[8,128]{1,0:T(8,128)}, f32[8,128]{1,0:T(8,128)}) custom-call(bf16[112,1024]{1,0:T(8,128)(2,1)} %tokens_ref.1, bf16[2,1024,1792]{2,1,0:T(8,128)(2,1)} %gate_up_ref.1, bf16[1792,1024]{1,0:T(8,128)(2,1)} %down_ref.1), custom_call_target="tpu_custom_call" | custom-call | tf_op jit(solution)/shard_map/swiglu_grid/pallas_call | solution.py:579
  91.9 1.7 %write_results.1 = (bf16[112,1024]{1,0:T(8,128)(2,1)}, f32[1024]{0:T(1024)}, f32[112]{0:T(128)}) custom-call(bf16[112,1024]{1,0:T(8,128)(2,1)} %get-tuple-element.6.mixed_ref, f32[8,128]{1,0:T(8,128)} %get-tuple-element.7.col_ref, f32[8,128]{1,0:T(8,128)} %get-tuple-element.8.row_ref), custom_call_target="tpu_custom_call" | custom-call | tf_op jit(solution)/shard_map/write_results/pallas_call | solution.py:617
